TPU v7x, 256 devices: a whole 4x4x8 slice. The times are simulated.
256 devices in a mesh: coils: 8 (over y, x_hi), slabs: 32 (over z, x_lo, core).
Axes of the slice: x: 4 (x_hi: 2, x_lo: 2; x = x_hi * 2 + x_lo), y: 4, z: 8, core: 2. Of those that a mesh axis runs over, the one named last changes fastest.
Arguments:
- kspace: float32 [2, 16, 96, 128, 256], P(None, 'coils', None, 'slabs'), may hold values from -6 to 6
- measured: float32 [2, 16, 24, 128, 256], P(None, 'coils', None, 'slabs'), may hold values from -6 to 6
- sampled_lines: int32 [24], replicated, may hold values from 0 to 95, as said below
- coil_maps: float32 [2, 16, 96, 128, 256], P(None, 'coils', 'slabs'), may hold values from -1.5 to 1.5
- step_size: float32 [1], replicated, may hold values from 0.5 to 2
- conv_one: bfloat16 [3, 3, 3, 18, 2], replicated, may hold values from -0.875 to 0.875
- bias_one: float32 [18], replicated, may hold values from -3 to 3
- conv_two: bfloat16 [3, 3, 3, 2, 18], replicated, may hold values from -0.25 to 0.25
- bias_two: float32 [2], replicated, may hold values from -3 to 3
- cotangent: float32 [2, 16, 96, 128, 256], P(None, 'coils', None, 'slabs'), may hold values from -0.006 to 0.006
Outputs:
- next_kspace: float32 [2, 16, 96, 128, 256], P(None, 'coils', None, 'slabs')
- grad_conv_one: float32 [3, 3, 3, 18, 2], replicated
- grad_bias_one: float32 [18], replicated
- grad_conv_two: float32 [3, 3, 3, 2, 18], replicated
- grad_bias_two: float32 [2], replicated
Inputs may be any that keep to these rules, and one draw needn't show every extreme that they name: `sampled_lines`: 24 distinct slice-encode positions; 0, 1, 94 and 95 are always among them.
All inputs are finite; a program needn't handle non-finite values.
Results may differ from a plain program's by a relative error of at most 0.0057.
Values may be sent and summed in bfloat16 or wider, within the bound.
A program may use at most 320 MiB of HBM per device.

v0:
```python
from types import SimpleNamespace

import jax
import jax.numpy as jnp
import ml_dtypes
import numpy as np
from jax import lax
from jax.experimental import pallas as pl
from jax.experimental.pallas import tpu as pltpu
from jax.sharding import PartitionSpec as P

NS, NP, NR, CH, LINES = 96, 128, 256, 18, 24
BF, F32 = jnp.bfloat16, jnp.float32
MESH = pl.DeviceIdType.MESH


def dft(n, direction):
    index = np.arange(n)
    angles = (np.outer(index, index) % n) * (2.0 * np.pi / n)
    return np.cos(angles) / np.sqrt(n), direction * np.sin(angles) / np.sqrt(n)


def split_np(table):
    high = table.astype(ml_dtypes.bfloat16)
    low = (table - high.astype(np.float64)).astype(ml_dtypes.bfloat16)
    return high, low


def readout_table(direction, passes):
    cos, sin = dft(NR, direction)
    high, low = split_np(np.concatenate([cos, sin], axis=1))
    return np.concatenate([high, high, low] if passes == 3 else [high, low], axis=0)


def slice_table(direction):
    cos, sin = dft(NS, direction)
    high, low = split_np(np.block([[cos, -sin], [sin, cos]]))
    return np.concatenate([high, high, low, np.zeros((192, 64))], axis=1)


def phase_table(direction):
    cos, sin = dft(NP, direction)
    pair = np.array([[cos, -sin], [sin, cos]])
    full = np.zeros((2, 2, NP, 2, 2, NP))
    for c in range(2):
        full[c, :, :, c] = pair.transpose(0, 2, 1, 3)
    return full


def phase_inverse():
    full = phase_table(1.0).reshape(512, 2, 2, 32, 4)
    ordered = full.transpose(0, 3, 1, 2, 4).reshape(512, 512)
    return np.concatenate(split_np(ordered), axis=1)


def phase_forward():
    full = phase_table(-1.0).reshape(2, 2, 32, 4, 512)
    ordered = full.transpose(2, 0, 1, 3, 4).reshape(512, 512)
    high, low = split_np(ordered)
    return np.concatenate([high, high, low], axis=1)


def edge_picks():
    pick = np.zeros((2, 16, 8, 16), np.float32)
    for plane in range(6):
        for k in range(2):
            pick[0, plane * 2 + k, plane, k] = 1
            pick[1, plane * 2 + k, plane, 14 + k] = 1
    return pick.reshape(32, 128)


def window_picks(planes):
    count = len(planes)
    rows = count * 32
    pick = np.zeros((count, 2, 24, 128), np.float32)
    for i, plane in enumerate(planes):
        for part in range(2):
            for t in range(2):
                pick[i, part, t, rows + (plane * 2 + part) * 2 + t] = 1
                pick[i, part, 18 + t, rows + 16 + (plane * 2 + part) * 2 + t] = 1
            for t in range(16):
                pick[i, part, 2 + t, (i * 2 + part) * 16 + t] = 1
    return pick.reshape(count * 48, 128)


def constants():
    rows = np.arange(432)
    col_p = rows % 24
    row_p = rows // 24
    band = np.full((432, 512), -100.0)
    band[:, :432] = col_p[None, :] - row_p[:, None]
    row_pick = np.zeros((432, 128), np.float32)
    row_pick[rows, rows % 24] = 1
    row_pick_t = np.zeros((32, 512), np.float32)
    row_pick_t[rows % 24, rows] = 1
    col_pick = np.zeros((128, 512), np.float32)
    col_pick[rows // 24, rows] = 1
    out_rows = np.arange(96)
    band_two = np.full((96, 512), -100.0)
    band_two[:, :432] = row_p[None, :] - (out_rows % 16)[:, None]
    out_pair = out_rows // 16
    pick_two = np.zeros((9, 96, 128), np.float32)
    pick_one = np.zeros((3, 128, 512), np.float32)
    pick_back = np.zeros((3, 128, 512), np.float32)
    group = rows // 24
    g_ds, g_dr, g_part = group // 6, group // 2 % 3, group % 2
    for at in range(9):
        pick_two[at, out_rows, 54 + (at * 3 + out_pair // 2) * 2 + out_pair % 2] = 1
    for dp in range(3):
        pick_one[dp, (g_ds * 9 + dp * 3 + g_dr) * 2 + g_part, rows] = 1
        flipped = ((2 - g_ds) * 9 + (2 - dp) * 3 + 2 - g_dr) * 2 + g_part
        pick_back[dp, 54 + flipped, rows] = 1
    col_pick_two = np.zeros((128, 512), np.float32)
    col_pick_two[rows % 24, rows] = 1
    staged = dict(
        rtab_inv=readout_table(1.0, 3),
        stab_inv=slice_table(1.0),
        ptab_inv=phase_inverse(),
        ptab_fwd=phase_forward(),
        rtab_fwd=readout_table(-1.0, 2),
        stab_fwd=slice_table(-1.0),
        band=band,
        pick_one=pick_one,
        pick_back=pick_back,
        pick_two=pick_two,
    )
    direct = dict(
        pick_edge=edge_picks(),
        pick_prev=window_picks((1, 2)),
        pick_own=window_picks((0, 1, 2)),
        pick_next=window_picks((0, 1)),
        row_pick=row_pick,
        band_two=band_two,
        col_pick_two=col_pick_two,
        row_pick_t=row_pick_t,
        col_pick_t=col_pick.T,
    )

    def low(table):
        return {k: jnp.asarray(np.asarray(v).astype(ml_dtypes.bfloat16)) for k, v in table.items()}

    return low(staged), low(direct)


def dot(a, b):
    return lax.dot_general(a, b, (((1,), (0,)), ((), ())), preferred_element_type=F32)


def dot_rows(a, b):
    return lax.dot_general(a, b, (((1,), (1,)), ((), ())), preferred_element_type=F32)


def split(value):
    high = value.astype(BF)
    return high, (value - high.astype(F32)).astype(BF)


def thirds(value):
    high, rest = value.astype(BF), value
    rest = rest - high.astype(F32)
    middle = rest.astype(BF)
    return high, middle, (rest - middle.astype(F32)).astype(BF)


def pick_rows(pick, value):
    return sum(dot(pick, piece) for piece in thirds(value))


def pick_cols(value, pick):
    return sum(dot(piece, pick) for piece in thirds(value))


def blank(rows, lanes=256):
    return jnp.zeros((rows, lanes), BF)


def deep(value, rows=512):
    return jnp.concatenate([value, blank(rows - value.shape[0], value.shape[1])], axis=0)


def with_ones(value):
    return jnp.concatenate([value, jnp.ones((80, 256), BF)], axis=0)


def low_half(shape, axis):
    return lax.broadcasted_iota(jnp.int32, shape, axis) < 4


def to_rows(even, odd):
    first = low_half(even.shape, 1)
    low = jnp.where(first, even, pltpu.roll(odd, 4, 1))
    high = jnp.where(first, pltpu.roll(even, 4, 1), odd)
    return low.reshape(-1, 128), high.reshape(-1, 128)


def from_rows(low, high):
    low = low.reshape(-1, 8, 128)
    high = high.reshape(-1, 8, 128)
    first = low_half(low.shape, 1)
    even = jnp.where(first, low, pltpu.roll(high, 4, 1))
    odd = jnp.where(first, pltpu.roll(low, 4, 1), high)
    return even, odd


def kernel(h, s, out_ref, one_ref, bias_one_ref, two_ref, bias_two_ref):
    coil = lax.axis_index("coils")
    slab = lax.axis_index("slabs")

    load = SimpleNamespace()
    for at, (name, source) in enumerate(vars(h).items()):
        copy = pltpu.make_async_copy(source, getattr(s.stage, name), s.load_sem.at[at])
        setattr(load, name, copy)
        copy.start()

    barrier = pltpu.get_barrier_semaphore()

    def greet(target_coil, target_slab):
        pl.semaphore_signal(
            barrier, inc=1, device_id=(target_coil, target_slab), device_id_type=MESH
        )

    @pl.loop(1, 32)
    def _(k):
        greet(coil, lax.rem(slab + k, 32))

    @pl.loop(1, 8)
    def _(k):
        greet(lax.rem(coil + k, 8), slab)

    @pl.loop(1, 8)
    def _(k):
        greet(lax.rem(coil + k, 8), slab + 1 - 2 * lax.rem(slab, 2))

    for dc in (1, 7):
        for ds in (1, 31):
            greet(lax.rem(coil + dc, 8), lax.rem(slab + ds, 32))

    def to_send(v, send, keep):
        rtab = s.stage.rtab_inv[...]
        stab = s.stage.stab_inv[...]
        z, y = s.z, s.y
        for c in range(2):
            uv = []
            for part in range(2):
                low, high = to_rows(v[part, c, :, 0], v[part, c, :, 1])
                if keep:
                    s.rows[0, part, c] = low
                    s.rows[1, part, c] = high
                x_high, x_low = split(jnp.concatenate([low, high], axis=1))
                uv.append(dot(jnp.concatenate([x_high, x_low, x_high], axis=1), rtab))
            z_real = uv[0][:, :256] - uv[1][:, 256:]
            z_imag = uv[1][:, :256] + uv[0][:, 256:]
            for half in range(2):
                lanes = slice(half * 128, half * 128 + 128)
                z[half, 0, c] = z_real[:, lanes]
                z[half, 1, c] = z_imag[:, lanes]
            for p in range(4):
                pick = pl.ds(p, 96, stride=4)
                parts = [
                    jnp.concatenate([z[0, part, c, pick, :], z[1, part, c, pick, :]], axis=1)
                    for part in range(2)
                ]
                z_high, z_low = split(jnp.concatenate(parts, axis=0))
                out = dot(stab, deep(jnp.concatenate([z_high, z_low, z_high], axis=0), 640))
                for part in range(2):
                    for half in range(2):
                        y[half, pl.ds(c * 8 + part * 4 + p, 96, stride=16), :] = out[
                            part * 96 : part * 96 + 96, half * 128 : half * 128 + 128
                        ]
        full = jnp.concatenate([y[0], y[1]], axis=1).astype(BF)
        send[...] = full.reshape(32, 48, 256)

    def exchange(send, recv, send_sem, recv_sem, first, last):
        @pl.loop(first, last)
        def _(k):
            target = lax.rem(slab + lax.rem(k * 13, 32), 32)
            pltpu.make_async_remote_copy(
                src_ref=send.at[target],
                dst_ref=recv.at[slab],
                send_sem=send_sem,
                recv_sem=recv_sem,
                device_id=(coil, target),
                device_id_type=MESH,
            ).start()

    def drained(ref, sem):
        pltpu.make_async_copy(ref, ref, sem).wait()

    def exchange_sent(send, send_sem):
        drained(send.at[pl.ds(0, 31)], send_sem)

    def exchange_arrived(recv, recv_sem):
        drained(recv.at[pl.ds(0, 31)], recv_sem)

    def combine(recv, part_own, rs_send, rs_recv, send_sem, recv_sem, low):
        table = s.stage.ptab_inv[...]
        maps = s.stage.maps
        for plane in range(3):
            values = recv[:, 16 * plane : 16 * plane + 16, :].reshape(512, 256)
            image = dot(table, jnp.concatenate([values, values], axis=0))
            real = jnp.zeros((128, 256), F32)
            imag = jnp.zeros((128, 256), F32)
            for c in range(2):
                m_real, m_imag = maps[0, c, plane], maps[1, c, plane]
                i_real = image[c * 256 : c * 256 + 128]
                i_imag = image[c * 256 + 128 : c * 256 + 256]
                real = real + m_real * i_real + m_imag * i_imag
                imag = imag + m_real * i_imag - m_imag * i_real
            part_own[:, plane, 0] = real.reshape(8, 16, 256)
            part_own[:, plane, 1] = imag.reshape(8, 16, 256)
            if low:
                rs_send[:, plane, 0] = real.astype(BF).reshape(8, 16, 256)
                rs_send[:, plane, 1] = imag.astype(BF).reshape(8, 16, 256)

        @pl.loop(1, 8)
        def _(k):
            target = lax.rem(coil + k, 8)
            pltpu.make_async_remote_copy(
                src_ref=rs_send.at[target],
                dst_ref=rs_recv.at[coil],
                send_sem=send_sem,
                recv_sem=recv_sem,
                device_id=(target, slab),
                device_id_type=MESH,
            ).start()

        rs_recv[coil] = jnp.zeros((3, 2, 16, 256), rs_recv.dtype)

    def combined(part_own, rs_send, rs_recv, send_sem, recv_sem):
        drained(rs_recv.at[pl.ds(0, 7)], recv_sem)
        drained(rs_send.at[pl.ds(0, 7)], send_sem)
        total = part_own[coil]
        for k in range(8):
            total = total + rs_recv[k].astype(F32)
        return total

    def halo_start(field, planes, edges, hp_recv, he_recv, sems):
        planes[...] = field.astype(BF).reshape(3, 32, 256)
        picked = dot(s.pick_edge[...], deep(planes[...].reshape(96, 256), 128))
        edges[...] = picked.astype(BF).reshape(2, 16, 256)
        prev, after = lax.rem(slab + 31, 32), lax.rem(slab + 1, 32)

        def send(src, dst, pair, target):
            pltpu.make_async_remote_copy(
                src_ref=src, dst_ref=dst, send_sem=sems.at[pair], recv_sem=sems.at[pair + 1],
                device_id=target, device_id_type=MESH,
            ).start()

        send(planes.at[pl.ds(1, 2)], hp_recv.at[0], 0, (coil, after))
        send(planes.at[pl.ds(0, 2)], hp_recv.at[1], 0, (coil, prev))
        for at, target_slab in ((2, prev), (1, slab), (0, after)):
            send(edges.at[1], he_recv.at[at, 0], 2, (lax.rem(coil + 1, 8), target_slab))
            send(edges.at[0], he_recv.at[at, 1], 2, (lax.rem(coil + 7, 8), target_slab))

    def halo_finish(planes, hp_recv, he_recv, sems, x):
        drained(hp_recv, sems.at[1])
        drained(he_recv, sems.at[3])
        drained(hp_recv, sems.at[0])
        drained(he_recv, sems.at[2])
        zero_edge = jnp.zeros((16, 256), BF)

        def group(body, at):
            lower = jnp.where(coil > 0, he_recv[at, 0], zero_edge)
            upper = jnp.where(coil < 7, he_recv[at, 1], zero_edge)
            return jnp.concatenate([body, lower, upper], axis=0)

        before = group(hp_recv[0].reshape(64, 256), 0)
        own = group(planes[...].reshape(96, 256), 1)
        after = group(hp_recv[1].reshape(64, 256), 2)
        before = dot(s.pick_prev[...], deep(before, 128))
        after = dot(s.pick_next[...], deep(after, 128))
        before = jnp.where(slab > 0, before, jnp.zeros_like(before))
        after = jnp.where(slab < 31, after, jnp.zeros_like(after))
        window = jnp.concatenate([before, dot(s.pick_own[...], own), after], axis=0)
        lane = lax.broadcasted_iota(jnp.int32, window.shape, 1)
        earlier = jnp.where(lane == 0, 0.0, pltpu.roll(window, 1, 1))
        later = jnp.where(lane == 255, 0.0, pltpu.roll(window, 255, 1))
        for dr, value in enumerate((earlier, window, later)):
            x[:, dr * 48 : dr * 48 + 48, :] = value.astype(BF).reshape(7, 48, 256)

    a2a = s.a2a_sem

    load.rtab_inv.wait()
    load.stab_inv.wait()
    load.kspace.wait()
    to_send(s.stage.kspace, s.send_one, True)
    pl.semaphore_wait(barrier, 49)
    exchange(s.send_one, s.recv_one, a2a.at[0], a2a.at[1], 1, 32)
    s.recv_one[slab] = s.send_one[slab]

    load.cotangent.wait()
    to_send(s.stage.cotangent, s.send_two, False)
    s.recv_two[slab] = s.send_two[slab]
    exchange(s.send_two, s.recv_two, a2a.at[2], a2a.at[3], 1, 32)

    load.band.wait()
    load.pick_one.wait()
    load.pick_back.wait()
    load.pick_two.wait()
    band = s.stage.band[...]
    row_pick = s.row_pick[...]
    s.taps[...] = jnp.zeros((128, 128), F32)
    for at in range(27):
        ds, dp, dr = at // 9, at // 3 % 3, at % 3
        s.taps[2 * at : 2 * at + 2, 0:CH] = s.conv_one[ds, dp, dr].astype(F32)
        s.taps[54 + 2 * at : 56 + 2 * at, 0:CH] = s.conv_two[ds, dp, dr].astype(F32)
    taps = s.taps[...].astype(BF)
    taps_t = s.taps[...].T.astype(BF)

    def banded(picks):
        total = jnp.zeros((432, 512), F32)
        for dp in range(3):
            tall = dot(row_pick, dot(taps_t, picks[dp]).astype(BF))
            total = total + jnp.where(band.astype(F32) == dp, tall, 0.0)
        return total.astype(BF)

    s.w_one[...] = banded(s.stage.pick_one)
    s.w_back[...] = banded(s.stage.pick_back)
    band_two = s.band_two[...]
    wide = dot(taps, s.col_pick_two[...]).astype(BF)
    for ds in range(3):
        total = jnp.zeros((96, 512), F32)
        for dp in range(3):
            tall = dot(s.stage.pick_two[ds * 3 + dp], wide)
            total = total + jnp.where(band_two.astype(F32) == dp, tall, 0.0)
        s.w_two[ds] = total.astype(BF)
    column = lax.broadcasted_iota(jnp.int32, (432, 128), 1)
    extra = blank(432, 128)
    row_b = lax.broadcasted_iota(jnp.int32, (128, 128), 0)
    bias = jnp.zeros((128, 128), F32)
    for at in range(CH):
        bias = jnp.where(row_b == at, s.bias_one[at], bias)
    for at, piece in enumerate(thirds(bias)):
        extra = jnp.where(column == 48 + at, dot(row_pick, piece), extra.astype(F32)).astype(BF)
    s.w_one[:, 384:512] = jnp.where(column >= 48, extra, s.w_one[:, 384:512])

    load.measured.wait()
    for part in range(2):
        for c in range(2):
            low, high = to_rows(s.stage.measured[part, c, :, 0], s.stage.measured[part, c, :, 1])
            s.meas_rows[0, part, c] = low
            s.meas_rows[1, part, c] = high

    exchange_arrived(s.recv_one, a2a.at[1])
    exchange_sent(s.send_one, a2a.at[0])
    load.ptab_inv.wait()
    load.maps.wait()
    rs_sem = s.rs_sem
    combine(s.recv_one, s.part_own, s.rs_send, s.rs_recv, rs_sem.at[0], rs_sem.at[1], True)
    image = combined(s.part_own, s.rs_send, s.rs_recv, rs_sem.at[0], rs_sem.at[1])
    halo = s.halo_sem
    halo_start(image, s.planes, s.edges, s.hp_recv, s.he_recv, halo.at[0])
    halo_finish(s.planes, s.hp_recv, s.he_recv, halo.at[0], s.x)

    x = s.x
    hidden = s.hidden
    row = lax.broadcasted_iota(jnp.int32, (432, 256), 0)
    inside = ((row >= 24) | (coil > 0)) & ((row < 408) | (coil < 7))
    own_rows = (row >= 24) & (row < 408)
    for plane in range(5):
        pre = dot(s.w_one[...], with_ones(x[plane : plane + 3].reshape(432, 256)))
        if 1 <= plane <= 3:
            s.pre[plane - 1] = pre
        value = pre / (1.0 + jnp.exp(-pre))
        keep = inside
        if plane == 0:
            keep = inside & (slab > 0)
        if plane == 4:
            keep = inside & (slab < 31)
        hidden[plane] = deep(jnp.where(keep, value, 0.0).astype(BF))
    lane = lax.broadcasted_iota(jnp.int32, (32, 256), 1)
    out_row = lax.broadcasted_iota(jnp.int32, (32, 256), 0)
    bias_two = jnp.where(out_row < 16, s.bias_two[0], s.bias_two[1])
    for plane in range(3):
        taps = jnp.zeros((96, 256), F32)
        for ds in range(3):
            taps = taps + dot(s.w_two[ds], hidden[plane + ds])
        earlier = jnp.where(lane == 0, 0.0, pltpu.roll(taps[0:32], 1, 1))
        later = jnp.where(lane == 255, 0.0, pltpu.roll(taps[64:96], 255, 1))
        update = earlier + taps[32:64] + later + bias_two
        s.ag_send[plane] = update.astype(BF)
    ag_sem = s.ag_sem

    @pl.loop(1, 8)
    def _(k):
        target = lax.rem(coil + k, 8)
        pltpu.make_async_remote_copy(
            src_ref=s.ag_send,
            dst_ref=s.ag_recv.at[coil],
            send_sem=ag_sem.at[0],
            recv_sem=ag_sem.at[1],
            device_id=(target, slab),
            device_id_type=MESH,
        ).start()

    s.ag_recv[coil] = s.ag_send[...]

    exchange_arrived(s.recv_two, a2a.at[3])
    exchange_sent(s.send_two, a2a.at[2])
    combine(s.recv_two, s.part_own, s.part_own, s.rs_recv_b, rs_sem.at[2], rs_sem.at[3], False)

    drained(s.ag_recv.at[pl.ds(0, 7)], ag_sem.at[1])
    drained(s.ag_recv.at[pl.ds(0, 7)], ag_sem.at[0])

    load.ptab_fwd.wait()
    for plane in range(3):
        u_real = s.ag_recv[:, plane, 0:16, :].reshape(128, 256).astype(F32)
        u_imag = s.ag_recv[:, plane, 16:32, :].reshape(128, 256).astype(F32)
        parts = []
        for c in range(2):
            m_real, m_imag = s.stage.maps[0, c, plane], s.stage.maps[1, c, plane]
            parts.append(m_real * u_real - m_imag * u_imag)
            parts.append(m_real * u_imag + m_imag * u_real)
        e_high, e_low = split(jnp.concatenate(parts, axis=0))
        out = dot(s.stage.ptab_fwd[...], jnp.concatenate([e_high, e_low, e_high], axis=0))
        s.send_three[:, plane * 16 : plane * 16 + 16, :] = out.astype(BF).reshape(32, 16, 256)
    exchange(s.send_three, s.recv_three, a2a.at[4], a2a.at[5], 1, 32)
    s.recv_three[slab] = s.send_three[slab]

    field = combined(s.part_own, s.part_own, s.rs_recv_b, rs_sem.at[2], rs_sem.at[3])
    halo_start(field, s.planes_b, s.edges_b, s.hp_recv_b, s.he_recv_b, halo.at[1])
    halo_finish(s.planes_b, s.hp_recv_b, s.he_recv_b, halo.at[1], s.xg)
    xg = s.xg
    band = s.stage.band[...]
    grad_one = jnp.zeros((432, 512), F32)
    grad_two = jnp.zeros((432, 512), F32)
    back_sum = jnp.zeros((432, 256), F32)
    for plane in range(3):
        near = deep(xg[plane + 1 : plane + 4].reshape(432, 256))
        back_hidden = dot(s.w_back[...], near)
        pre = s.pre[plane]
        sigmoid = 1.0 / (1.0 + jnp.exp(-pre))
        back = back_hidden * sigmoid * (1.0 + pre * (1.0 - sigmoid))
        back = jnp.where(own_rows, back, 0.0)
        back_sum = back_sum + back
        grad_one = grad_one + dot_rows(
            back.astype(BF), deep(x[plane + 1 : plane + 4].reshape(432, 256))
        )
        mine = jnp.where(own_rows, hidden[plane + 1, :432], blank(432))
        grad_two = grad_two + dot_rows(mine, near)
    row_pick_t = s.row_pick_t[...]
    col_pick_t = s.col_pick_t[...]
    pack = jnp.zeros((32, 128), F32)
    for first, grad in ((0, grad_one), (54, grad_two)):
        pieces = split(grad)
        for dp in range(3):
            on_band = band == dp
            left = jnp.zeros((32, 512), F32)
            for piece in pieces:
                left = left + dot(row_pick_t, deep(jnp.where(on_band, piece, blank(432, 512))))
            piece = pick_cols(left, col_pick_t)
            at = first + 18 * dp
            pack = pack + (pltpu.roll(piece, at, 1) if at else piece)
    lane_p = lax.broadcasted_iota(jnp.int32, (32, 128), 1)
    row_p = lax.broadcasted_iota(jnp.int32, (32, 128), 0)
    bias_grad = sum(dot(row_pick_t, deep(piece)) for piece in split(back_sum))
    bias_grad = jnp.sum(bias_grad, axis=1, keepdims=True)
    pack = pack + jnp.where(lane_p == 108, bias_grad, 0.0)
    real_sum = jnp.sum(field[:, 0])
    imag_sum = jnp.sum(field[:, 1])
    pack = pack + jnp.where(
        lane_p == 109, jnp.where(row_p == 0, real_sum, jnp.where(row_p == 1, imag_sum, 0.0)), 0.0
    )
    sum_send, sum_sem = s.sum_send, s.sum_sem
    sum_send[0] = pack[:24]

    def spread_start(stage, recv, size, mine, target_of):
        recv[mine] = sum_send[stage]

        @pl.loop(1, size)
        def _(k):
            pltpu.make_async_remote_copy(
                src_ref=sum_send.at[stage],
                dst_ref=recv.at[mine],
                send_sem=sum_sem.at[2 * stage],
                recv_sem=sum_sem.at[2 * stage + 1],
                device_id=target_of(k),
                device_id_type=MESH,
            ).start()

    def spread_end(stage, recv, size):
        drained(recv.at[pl.ds(0, size - 1)], sum_sem.at[2 * stage + 1])
        drained(recv.at[pl.ds(0, size - 1)], sum_sem.at[2 * stage])

    def added(recv, size):
        total = recv[0]
        for k in range(1, size):
            total = total + recv[k]
        return total

    core = lax.rem(slab, 2)
    place_one = coil * 2 + core

    def target_one(k):
        to = lax.rem(place_one + k, 16)
        return lax.div(to, 2), slab - core + lax.rem(to, 2)

    spread_start(0, s.sum_near, 16, place_one, target_one)
    spread_end(0, s.sum_near, 16)
    sum_send[1] = added(s.sum_near, 16)
    spread_start(1, s.sum_far, 16, lax.div(slab, 2), lambda k: (coil, lax.rem(slab + 2 * k, 32)))

    load.rtab_fwd.wait()
    load.stab_fwd.wait()
    step = s.step[0]
    row_o = lax.broadcasted_iota(jnp.int32, (192, 128), 0)
    col_o = lax.broadcasted_iota(jnp.int32, (192, 128), 1)
    slice_o = jnp.where(row_o >= 96, row_o - 96, row_o)
    col_imag = ((col_o >= 24) & (col_o < 48)) | (col_o >= 72)
    col_l = lax.broadcasted_iota(jnp.int32, (8, 128), 1)
    line_l = jnp.full((8, 128), -1, jnp.int32)
    for at in range(LINES):
        here = (col_l == at) | (col_l == at + 24) | (col_l == at + 48) | (col_l == at + 72)
        line_l = jnp.where(here, s.lines[at], line_l)
    picked = (slice_o == line_l[0:1]) & ((row_o >= 96) == col_imag)
    place = jnp.where(picked, 1.0, 0.0)
    keep = 1.0 - step * 0.5 * jnp.sum(place, axis=1, keepdims=True)
    place = place.astype(BF)
    exchange_arrived(s.recv_three, a2a.at[5])
    exchange_sent(s.send_three, a2a.at[4])
    z, y = s.z, s.y
    first = low_half((48, 8, 256), 1)
    for chunk in range(4):
        values = s.recv_three[chunk * 8 : chunk * 8 + 8].reshape(384, 256)
        uv = dot(jnp.concatenate([values, values], axis=1), s.stage.rtab_fwd[...])
        u = uv[:, :256].reshape(48, 8, 256)
        v = pltpu.roll(uv[:, 256:].reshape(48, 8, 256), 4, 1)
        full = (u + jnp.where(first, -v, v)).reshape(384, 256)
        y[0, chunk * 384 : chunk * 384 + 384, :] = full[:, :128]
        y[1, chunk * 384 : chunk * 384 + 384, :] = full[:, 128:]
    for c in range(2):
        for p in range(4):
            parts, lines, held = [], [], []
            for part in range(2):
                pick = pl.ds(c * 8 + part * 4 + p, 96, stride=16)
                parts.append(jnp.concatenate([y[0, pick, :], y[1, pick, :]], axis=1))
                pick = pl.ds(p, 24, stride=4)
                lines.append(
                    jnp.concatenate(
                        [s.meas_rows[half, part, c, pick, :] for half in range(2)], axis=1
                    )
                )
                pick = pl.ds(p, 96, stride=4)
                held.append(
                    jnp.concatenate(
                        [s.rows[half, part, c, pick, :] for half in range(2)], axis=1
                    )
                )
            z_high, z_low = split(jnp.concatenate(parts, axis=0))
            out = dot(s.stage.stab_fwd[...], deep(jnp.concatenate([z_high, z_low, z_high], axis=0), 640))
            m_high, m_low = split(step * jnp.concatenate(lines, axis=0))
            out = out + dot(place, jnp.concatenate([m_high, m_low, blank(32)], axis=0))
            out = out + keep * jnp.concatenate(held, axis=0)
            pick = pl.ds(p, 96, stride=4)
            for part in range(2):
                for half in range(2):
                    z[half, part, c, pick, :] = out[
                        part * 96 : part * 96 + 96, half * 128 : half * 128 + 128
                    ]
        for part in range(2):
            even, odd = from_rows(z[0, part, c], z[1, part, c])
            out_ref[part, c, :, 0] = even
            out_ref[part, c, :, 1] = odd

    spread_end(1, s.sum_far, 16)
    total = jnp.concatenate([added(s.sum_far, 16), jnp.zeros((104, 128), F32)], axis=0)
    s.taps[...] = total.T
    for at in range(27):
        ds, dp, dr = at // 9, at // 3 % 3, at % 3
        row = dp * 18 + (ds * 3 + dr) * 2
        one_ref[ds, dp, dr] = s.taps[row : row + 2, 0:CH]
        two_ref[2 - ds, 2 - dp, 2 - dr] = s.taps[54 + row : 56 + row, 0:CH]
    bias_one_ref[...] = s.taps[108:109, 0:CH]
    bias_two_ref[...] = s.taps[109:110, 0:2]


def tiles(values):
    count = values.shape[2]
    split_lanes = values.reshape(2, 2, count, 4, 2, 128).transpose(0, 1, 2, 4, 3, 5)
    return split_lanes.reshape(2, 2, count // 2, 2, 8, 128)


def untiles(values):
    split_lanes = values.reshape(2, 2, 96, 2, 4, 128).transpose(0, 1, 2, 4, 3, 5)
    return split_lanes.reshape(2, 2, 96, 4, 256)


def body(kspace, measured, sampled_lines, coil_maps, step_size, conv_one, bias_one, conv_two,
         bias_two, cotangent):
    staged_tables, direct_tables = constants()
    staged = dict(
        rtab_inv=staged_tables.pop("rtab_inv"),
        kspace=tiles(kspace),
        stab_inv=staged_tables.pop("stab_inv"),
        cotangent=tiles(cotangent),
        measured=tiles(measured),
        maps=coil_maps,
        **staged_tables,
    )
    direct = dict(
        conv_one=conv_one.transpose(0, 1, 2, 4, 3),
        conv_two=conv_two,
        **direct_tables,
    )
    scalars = dict(step=step_size, bias_two=bias_two, bias_one=bias_one, lines=sampled_lines)
    spectra = pltpu.VMEM((32, 48, 256), BF)
    parts = pltpu.VMEM((8, 3, 2, 16, 256), BF)
    planes = pltpu.VMEM((3, 32, 256), BF)
    edges = pltpu.VMEM((2, 16, 256), BF)
    hp_recv = pltpu.VMEM((2, 2, 32, 256), BF)
    he_recv = pltpu.VMEM((3, 2, 16, 256), BF)
    scratch = dict(
        load_sem=pltpu.SemaphoreType.DMA((len(staged),)),
        rows=pltpu.VMEM((2, 2, 2, 384, 128), F32),
        meas_rows=pltpu.VMEM((2, 2, 2, 96, 128), F32),
        z=pltpu.VMEM((2, 2, 2, 384, 128), F32),
        y=pltpu.VMEM((2, 1536, 128), F32),
        a2a_sem=pltpu.SemaphoreType.DMA((6,)),
        part_own=pltpu.VMEM((8, 3, 2, 16, 256), F32),
        rs_sem=pltpu.SemaphoreType.DMA((4,)),
        x=pltpu.VMEM((7, 144, 256), BF),
        xg=pltpu.VMEM((7, 144, 256), BF),
        halo_sem=pltpu.SemaphoreType.DMA((2, 4)),
        taps=pltpu.VMEM((128, 128), F32),
        w_one=pltpu.VMEM((432, 512), BF),
        w_back=pltpu.VMEM((432, 512), BF),
        w_two=pltpu.VMEM((3, 96, 512), BF),
        hidden=pltpu.VMEM((5, 512, 256), BF),
        pre=pltpu.VMEM((3, 432, 256), F32),
        ag_send=pltpu.VMEM((3, 32, 256), BF),
        ag_recv=pltpu.VMEM((8, 3, 32, 256), BF),
        ag_sem=pltpu.SemaphoreType.DMA((2,)),
        sum_send=pltpu.VMEM((2, 24, 128), F32),
        sum_near=pltpu.VMEM((16, 24, 128), F32),
        sum_far=pltpu.VMEM((16, 24, 128), F32),
        sum_sem=pltpu.SemaphoreType.DMA((4,)),
        send_one=spectra,
        send_two=spectra,
        send_three=spectra,
        recv_one=spectra,
        recv_two=spectra,
        recv_three=spectra,
        rs_send=parts,
        rs_recv=parts,
        rs_recv_b=pltpu.VMEM((8, 3, 2, 16, 256), F32),
        planes=planes,
        planes_b=planes,
        edges=edges,
        edges_b=edges,
        hp_recv=hp_recv,
        hp_recv_b=hp_recv,
        he_recv=he_recv,
        he_recv_b=he_recv,
    )
    stage = [pltpu.VMEM(value.shape, value.dtype) for value in staged.values()]

    def entry(*refs):
        refs = list(refs)

        def take(table):
            return {key: refs.pop(0) for key in table}

        h = SimpleNamespace(**take(staged))
        own = take(direct)
        own.update(take(scalars))
        outs = [refs.pop(0) for _ in range(5)]
        own.update(take(scratch))
        kernel(h, SimpleNamespace(**own, stage=SimpleNamespace(**take(staged))), *outs)

    in_vmem = pl.BlockSpec(memory_space=pltpu.VMEM)
    out, grad_one, grad_bias_one, grad_two, grad_bias_two = pl.pallas_call(
        entry,
        out_shape=(
            jax.ShapeDtypeStruct((2, 2, 48, 2, 8, 128), F32),
            jax.ShapeDtypeStruct((3, 3, 3, 2, CH), F32),
            jax.ShapeDtypeStruct((1, CH), F32),
            jax.ShapeDtypeStruct((3, 3, 3, 2, CH), F32),
            jax.ShapeDtypeStruct((1, 2), F32),
        ),
        in_specs=[pl.BlockSpec(memory_space=pl.ANY)] * len(staged)
        + [in_vmem] * len(direct)
        + [pl.BlockSpec(memory_space=pltpu.SMEM)] * len(scalars),
        out_specs=(in_vmem,) * 5,
        scratch_shapes=list(scratch.values()) + stage,
        compiler_params=pltpu.CompilerParams(
            collective_id=0, has_side_effects=True, vmem_limit_bytes=56 * 1024 * 1024
        ),
        name="cascade",
    )(*staged.values(), *direct.values(), *scalars.values())

    return (
        untiles(out),
        grad_one.transpose(0, 1, 2, 4, 3),
        grad_bias_one.reshape(CH),
        grad_two,
        grad_bias_two.reshape(2),
    )


def solution(mesh):
    kspace = P(None, "coils", None, "slabs", None)
    placed = (
        kspace,
        kspace,
        P(),
        P(None, "coils", "slabs", None, None),
        P(),
        P(),
        P(),
        P(),
        P(),
        kspace,
    )
    return jax.shard_map(
        body,
        mesh=mesh,
        in_specs=placed,
        out_specs=(kspace, P(), P(), P(), P()),
        check_vma=False,
    )
```

profile of v0, /device:TPU:1, one launch (start us, length us, event | category | flops | bytes accessed | tf_op | source)
XLA Modules:
  0.0 105.3 jit_solution(10661021525536769565)
XLA Ops:
  1.3 98.9 %cascade.1 = (f32[2,2,48,2,8,128]{5,4,3,2,1,0:T(8,128)}, f32[3,3,3,2,18]{4,3,2,1,0:T(2,128)}, f32[1,18]{1,0:T(1,128)}, f32[3,3,3,2,18]{4,3,2,1,0:T(2,128)}, f32[1,2]{1,0:T(1,128)}) custom-call(bf16[768,512]{1,0:T(8,128)(2,1)} %constant.38.clone.refs_0_, f32[2,2,48,2,8,128]{5,4,3,2,1,0:T(8,128)} %bitcast.24, bf16[192,640]{1,0:T(8,128)(2,1)} %constant.39.clone.refs_2_, ...), custom_call_target="tpu_custom_call" | custom-call | tf_op jit(solution)/shard_map/cascade/pallas_call | solution.py:771
  100.1 0.0 copy-start.1
  100.1 0.0 copy-start.3
  100.2 0.0 copy-start
  100.2 0.0 copy-start.2
  100.2 2.8 %copy.44 = f32[2,2,96,4,256]{4,3,2,1,0:T(4,128)} copy(f32[2,2,96,4,256]{4,3,2,1,0:T(4,128)} %bitcast.26) | data formatting | bytes 3145728
  103.0 0.0 copy-done.1
  103.0 0.6 copy.45
  103.6 0.0 copy-done.3
  103.6 0.5 copy.46
  104.1 0.0 copy-done
  104.1 0.6 copy.47
  104.7 0.0 copy-done.2
  104.7 0.5 copy.48
Async XLA Ops:
  100.1 2.9 %copy-start.1 = (f32[3,3,3,2,18]{4,3,2,1,0:T(2,128)S(1)}, f32[3,3,3,2,18]{4,3,2,1,0:T(2,128)}, u32[]{:S(2)}) copy-start(f32[3,3,3,2,18]{4,3,2,1,0:T(2,128)} %get-tuple-element.11) | copy-start | bytes 11668
  100.1 3.5 %copy-start.3 = (f32[1,18]{1,0:T(1,128)S(1)}, f32[1,18]{1,0:T(1,128)}, u32[]{:S(2)}) copy-start(f32[1,18]{1,0:T(1,128)} %get-tuple-element.12) | copy-start | bytes 220
  100.2 4.0 %copy-start = (f32[3,3,3,2,18]{4,3,2,1,0:T(2,128)S(1)}, f32[3,3,3,2,18]{4,3,2,1,0:T(2,128)}, u32[]{:S(2)}) copy-start(f32[3,3,3,2,18]{4,3,2,1,0:T(2,128)} %get-tuple-element.23) | copy-start | bytes 11668
  100.2 4.6 %copy-start.2 = (f32[1,2]{1,0:T(1,128)S(1)}, f32[1,2]{1,0:T(1,128)}, u32[]{:S(2)}) copy-start(f32[1,2]{1,0:T(1,128)} %get-tuple-element.14) | copy-start | bytes 28
where the time goes:
time: 106 us; the launch traced here: 105 us
  Pallas kernels  98.9 us (93%)
  local copies, waits for them, and re-layouts  5.08 us (5%)
  between operations  1.32 us (1%)
    pallas_call x1, Pallas kernels, body(): pl.pallas_call(entry, out_shape=(jax.ShapeDtypeStruct((2, 2, 48, 2, 8, 12...  98.9 us
    unnamed x13, local copies, waits for them, and re-layouts  5.08 us

commit v1 on v0

--- a/solution.py
+++ b/solution.py
@@ -450,6 +450,10 @@
     image = combined(s.part_own, s.rs_send, s.rs_recv, rs_sem.at[0], rs_sem.at[1])
     halo = s.halo_sem
     halo_start(image, s.planes, s.edges, s.hp_recv, s.he_recv, halo.at[0])
+    exchange_arrived(s.recv_two, a2a.at[3])
+    exchange_sent(s.send_two, a2a.at[2])
+    combine(s.recv_two, s.part_own, s.part_own, s.rs_recv_b, rs_sem.at[2], rs_sem.at[3], False)
+
     halo_finish(s.planes, s.hp_recv, s.he_recv, halo.at[0], s.x)
 
     x = s.x
@@ -495,10 +499,6 @@
 
     s.ag_recv[coil] = s.ag_send[...]
 
-    exchange_arrived(s.recv_two, a2a.at[3])
-    exchange_sent(s.send_two, a2a.at[2])
-    combine(s.recv_two, s.part_own, s.part_own, s.rs_recv_b, rs_sem.at[2], rs_sem.at[3], False)
-
     drained(s.ag_recv.at[pl.ds(0, 7)], ag_sem.at[1])
     drained(s.ag_recv.at[pl.ds(0, 7)], ag_sem.at[0])
 
@@ -514,11 +514,11 @@
         e_high, e_low = split(jnp.concatenate(parts, axis=0))
         out = dot(s.stage.ptab_fwd[...], jnp.concatenate([e_high, e_low, e_high], axis=0))
         s.send_three[:, plane * 16 : plane * 16 + 16, :] = out.astype(BF).reshape(32, 16, 256)
+    field = combined(s.part_own, s.part_own, s.rs_recv_b, rs_sem.at[2], rs_sem.at[3])
+    halo_start(field, s.planes_b, s.edges_b, s.hp_recv_b, s.he_recv_b, halo.at[1])
     exchange(s.send_three, s.recv_three, a2a.at[4], a2a.at[5], 1, 32)
     s.recv_three[slab] = s.send_three[slab]
 
-    field = combined(s.part_own, s.part_own, s.rs_recv_b, rs_sem.at[2], rs_sem.at[3])
-    halo_start(field, s.planes_b, s.edges_b, s.hp_recv_b, s.he_recv_b, halo.at[1])
     halo_finish(s.planes_b, s.hp_recv_b, s.he_recv_b, halo.at[1], s.xg)
     xg = s.xg
     band = s.stage.band[...]
@@ -788,6 +788,19 @@
         name="cascade",
     )(*staged.values(), *direct.values(), *scalars.values())
 
+    results = (out, grad_one, grad_bias_one, grad_two, grad_bias_two)
+
+    def hand_over(*refs):
+        for at in range(5):
+            refs[5 + at][...] = refs[at][...]
+
+    out, grad_one, grad_bias_one, grad_two, grad_bias_two = pl.pallas_call(
+        hand_over,
+        out_shape=tuple(jax.ShapeDtypeStruct(r.shape, r.dtype) for r in results),
+        in_specs=[in_vmem] * 5,
+        out_specs=(in_vmem,) * 5,
+        name="results",
+    )(*results)
     return (
         untiles(out),
         grad_one.transpose(0, 1, 2, 4, 3),

time: 106 us -> 98.1 us (0.925)
  local copies, waits for them, and re-layouts: 5.08 us -> 0 us
  Pallas kernels: 98.9 us -> 96.7 us
    unnamed x13 -> x0, local copies, waits for them, and re-layouts: 5.08 us -> none
    pallas_call x1, Pallas kernels: 98.9 us -> 94 us  [body(): pl.pallas_call(entry, out_shape=(jax.ShapeDtypeStruct((2, 2, 48, 2, 8, 12...]
    pallas_call x0 -> x1, Pallas kernels: none -> 2.72 us  [body(): pl.pallas_call(hand_over, out_shape=tuple((jax.ShapeDtypeStruct(r.shape,...]
where the time goes in v1:
time: 98.1 us; the launch traced here: 98 us
  Pallas kernels  96.7 us (99%)
  between operations  1.29 us (1%)
    pallas_call x1, Pallas kernels, body(): pl.pallas_call(entry, out_shape=(jax.ShapeDtypeStruct((2, 2, 48, 2, 8, 12...  94 us
    pallas_call x1, Pallas kernels, body(): pl.pallas_call(hand_over, out_shape=tuple((jax.ShapeDtypeStruct(r.shape,...  2.72 us

profile of v1, /device:TPU:1, one launch (start us, length us, event | category | flops | bytes accessed | tf_op | source)
XLA Modules:
  0.0 98.0 jit_solution(11467251335582482178)
XLA Ops:
  1.3 94.0 %cascade.1 = (f32[2,2,48,2,8,128]{5,4,3,2,1,0:T(8,128)}, f32[3,3,3,2,18]{4,3,2,1,0:T(2,128)}, f32[1,18]{1,0:T(1,128)}, f32[3,3,3,2,18]{4,3,2,1,0:T(2,128)}, f32[1,2]{1,0:T(1,128)}) custom-call(bf16[768,512]{1,0:T(8,128)(2,1)} %constant.38.clone.refs_0_, f32[2,2,48,2,8,128]{5,4,3,2,1,0:T(8,128)} %bitcast.24, bf16[192,640]{1,0:T(8,128)(2,1)} %constant.39.clone.refs_2_, ...), custom_call_target="tpu_custom_call" | custom-call | tf_op jit(solution)/shard_map/cascade/pallas_call | solution.py:771
  95.3 2.7 %results.1 = (f32[2,2,48,2,8,128]{5,4,3,2,1,0:T(8,128)}, f32[3,3,3,2,18]{4,3,2,1,0:T(2,128)}, f32[1,18]{1,0:T(1,128)}, f32[3,3,3,2,18]{4,3,2,1,0:T(2,128)}, f32[1,2]{1,0:T(1,128)}) custom-call(f32[2,2,48,2,8,128]{5,4,3,2,1,0:T(8,128)} %get-tuple-element.15.refs_0_, f32[3,3,3,2,18]{4,3,2,1,0:T(2,128)} %get-tuple-element.16.refs_1_, ...), custom_call_target="tpu_custom_call" | custom-call | tf_op jit(solution)/shard_map/results/pallas_call | solution.py:797
